TPU v7x, 32 devices: a whole 2x2x4 slice. The times are simulated.
32 devices in a mesh: groups: 2 (over x), seq: 16 (over z, y, core).
Axes of the slice: x: 2, y: 2, z: 4, core: 2. Of those that a mesh axis runs over, the one named last changes fastest.
Arguments:
- hidden: bfloat16 [12288, 3072], P(('groups', 'seq')), parts along dimension 0, may hold values from -6 to 6
- query_rows: bfloat16 [12288, 1536], P(('groups', 'seq')), parts along dimension 0, may hold values from -200 to 200
- key_rows: bfloat16 [12288, 1536], P(('groups', 'seq')), parts along dimension 0, may hold values from -10 to 10
- value_rows: bfloat16 [12288, 1536], P(('groups', 'seq')), parts along dimension 0, may hold values from -6 to 6
- out_weight: bfloat16 [1536, 3072], replicated, may hold values from -1.25 to 1.25
- masked_tiles: int32 [24], P('groups'), parts along dimension 0, may hold values from 0 to 47, as said below
Outputs:
- painted: bfloat16 [12288, 3072], P(('groups', 'seq')), parts along dimension 0
There are 2 independent parts, one for each index of `groups`. A program takes and returns all parts, laid end to end along the dimension named above; an argument that names none is the same for every part. Nothing has to cross between parts.
Inputs may be any that keep to these rules, and one draw needn't show every extreme that they name: `masked_tiles`: 12 distinct tile indices in increasing order; in every clip all 3 tiles of one index of seq (tiles d * 3 to (d + 1) * 3 - 1) are masked.
All inputs are finite; a program needn't handle non-finite values.
Results may differ from a plain program's by a relative error of at most 0.0065.
Values may be sent and summed in bfloat16 or wider, within the bound.
A program may use at most 128 MiB of HBM per device.

v0:
```python
import math

import jax
import jax.numpy as jnp
from jax import lax
from jax.sharding import PartitionSpec as P

HEADS = 24
TILE = 128
TILES_DEV = 3


very_low = -1e30


def layout(masked_tiles, devices, device):
    slot_ids = jnp.arange(TILES_DEV, dtype=jnp.int32)
    local_ids = device * TILES_DEV + slot_ids
    is_masked = jnp.any(masked_tiles[None, :] == local_ids[:, None], axis=1).astype(jnp.int32)
    rank_here = jnp.cumsum(is_masked) - is_masked
    count_here = jnp.sum(is_masked)
    chosen = (rank_here[None, :] == slot_ids[:, None]) & (is_masked[None, :] == 1)
    source_tile = jnp.sum(jnp.where(chosen, slot_ids[None, :], 0), axis=1)
    slot_live = (slot_ids < count_here).astype(jnp.int32)
    owners = jnp.arange(devices, dtype=jnp.int32)
    home_device = masked_tiles // TILES_DEV
    per_source = jnp.sum((home_device[None, :] == owners[:, None]).astype(jnp.int32), axis=1)
    return (is_masked, rank_here, source_tile, slot_live, per_source)


def pack(field, source_tile, slot_live, devices):
    width = field.shape[1]
    tiles = field.reshape(TILES_DEV, TILE, width)
    picked = jnp.take(tiles, source_tile, axis=0) * slot_live[:, None, None].astype(field.dtype)
    return picked.reshape(TILES_DEV * TILE // devices, devices, width)


def dense_index(per_source, devices, own_rows):
    per_row = per_source * (TILE // devices)
    ends = jnp.cumsum(per_row)
    starts = ends - per_row
    positions = jnp.arange(own_rows, dtype=jnp.int32)
    source_of = jnp.sum((ends[None, :] <= positions[:, None]).astype(jnp.int32), axis=1)
    owners = jnp.arange(devices, dtype=jnp.int32)
    start_of = jnp.sum(jnp.where(owners[None, :] == source_of[:, None], starts[None, :], 0), axis=1)
    return (positions - start_of) * devices + source_of


def take_dense(received, gather_rows):
    flat = received.reshape(received.shape[0] * received.shape[1], received.shape[2])
    return jnp.take(flat, gather_rows, axis=0)


def attend(queries, keys_own, values_own):
    row_count = queries.shape[0]
    head_dim = queries.shape[1] // HEADS
    query_grid = queries.reshape(row_count, HEADS, head_dim)
    scale = 1.0 / math.sqrt(head_dim)
    start_state = (
        jnp.full((HEADS, row_count), very_low, jnp.float32),
        jnp.zeros((HEADS, row_count), jnp.float32),
        jnp.zeros((HEADS, row_count, head_dim), jnp.float32),
    )
    key_piece = lax.all_gather(keys_own, "seq", axis=0, tiled=True)
    value_piece = lax.all_gather(values_own, "seq", axis=0, tiled=True)
    length = key_piece.shape[0]
    block = math.gcd(length, 512)

    def one_block(index_block, state):
        best, total, summed = state
        key_block = lax.dynamic_slice_in_dim(key_piece, index_block * block, block, 0).reshape(
            block, HEADS, head_dim
        )
        value_block = lax.dynamic_slice_in_dim(value_piece, index_block * block, block, 0).reshape(
            block, HEADS, head_dim
        )
        scores = (
            jnp.einsum("qhd,khd->hqk", query_grid, key_block, preferred_element_type=jnp.float32)
            * scale
        )
        new_best = jnp.maximum(best, jnp.max(scores, axis=2))
        fade = jnp.exp(best - new_best)
        weights = jnp.exp(scores - new_best[:, :, None])
        total = total * fade + jnp.sum(weights, axis=2)
        summed = summed * fade[:, :, None] + jnp.einsum(
            "hqk,khd->hqd",
            weights.astype(jnp.bfloat16),
            value_block,
            preferred_element_type=jnp.float32,
        )
        return (new_best, total, summed)

    best, total, summed = lax.fori_loop(0, length // block, one_block, start_state)
    result = summed / total[:, :, None]
    return (
        jnp.transpose(result, (1, 0, 2)).reshape(row_count, HEADS * head_dim).astype(jnp.bfloat16)
    )


def body(hidden, query_rows, key_rows, value_rows, out_weight, masked_tiles):
    devices = lax.axis_size("seq")
    device = lax.axis_index("seq")
    is_masked, rank_here, source_tile, slot_live, per_source = layout(masked_tiles, devices, device)
    own_rows = masked_tiles.shape[0] * TILE // devices
    gather_rows = dense_index(per_source, devices, own_rows)
    sent = (
        pack(key_rows, source_tile, slot_live, devices),
        pack(value_rows, source_tile, slot_live, devices),
    )
    got_key, got_value = (
        lax.all_to_all(sent[0], "seq", split_axis=1, concat_axis=1, tiled=True),
        lax.all_to_all(sent[1], "seq", split_axis=1, concat_axis=1, tiled=True),
    )
    attended = attend(
        query_rows, take_dense(got_key, gather_rows), take_dense(got_value, gather_rows)
    )
    row_mask = jnp.repeat(is_masked, TILE).astype(jnp.float32)
    projected = jnp.dot(attended, out_weight, preferred_element_type=jnp.float32).astype(
        jnp.bfloat16
    )
    placed = projected * row_mask[:, None].astype(jnp.bfloat16)
    painted = hidden.astype(jnp.float32) + placed.astype(jnp.float32)
    return painted.astype(jnp.bfloat16)


def solution(mesh):
    placed = (
        P(("groups", "seq"), None),
        P(("groups", "seq"), None),
        P(("groups", "seq"), None),
        P(("groups", "seq"), None),
        P(),
        P("groups"),
    )
    return jax.shard_map(
        body, mesh=mesh, in_specs=placed, out_specs=P(("groups", "seq"), None), check_vma=False
    )
```

profile of v0, /device:TPU:0, one launch (start us, length us, event | category | flops | bytes accessed | tf_op | source)
XLA Modules:
  0.0 318.6 jit_solution(10532076719937441505)
XLA Ops:
  12.4 7.4 %all-to-all-start = ((bf16[24,16,1536]{2,0,1:T(8,128)(2,1)}), bf16[24,16,1536]{2,0,1:T(8,128)(2,1)S(1)}, u32[]{:S(2)}, u32[]{:S(2)}) async-start(bf16[24,16,1536]{2,0,1:T(8,128)(2,1)} %copy.35), calls=%async_computation | async-start | bytes 2359296 | tf_op jit(solution)/shard_map/all_to_all | solution.py:111
  21.4 23.5 %all-to-all-done = bf16[24,16,1536]{2,0,1:T(8,128)(2,1)S(1)} async-done(((bf16[24,16,1536]{2,0,1:T(8,128)(2,1)}), bf16[24,16,1536]{2,0,1:T(8,128)(2,1)S(1)}, u32[]{:S(2)}, u32[]{:S(2)}) %all-to-all-start) | async-done | bytes 1179680 | tf_op jit(solution)/shard_map/all_to_all | solution.py:111
  44.9 7.5 %all-to-all-start.1 = ((bf16[24,16,1536]{2,0,1:T(8,128)(2,1)}), bf16[24,16,1536]{2,0,1:T(8,128)(2,1)S(1)}, u32[]{:S(2)}, u32[]{:S(2)}) async-start(bf16[24,16,1536]{2,0,1:T(8,128)(2,1)} %copy.38), calls=%async_computation.1 | async-start | bytes 2359296 | tf_op jit(solution)/shard_map/all_to_all | solution.py:112
  54.9 22.6 %all-to-all-done.1 = bf16[24,16,1536]{2,0,1:T(8,128)(2,1)S(1)} async-done(((bf16[24,16,1536]{2,0,1:T(8,128)(2,1)}), bf16[24,16,1536]{2,0,1:T(8,128)(2,1)S(1)}, u32[]{:S(2)}, u32[]{:S(2)}) %all-to-all-start.1) | async-done | bytes 1179680 | tf_op jit(solution)/shard_map/all_to_all | solution.py:112
  81.4 54.7 %all-gather.3.cloned.1.call-done = bf16[1536,1536]{1,0:T(8,128)(2,1)} async-done(((bf16[96,1536]{1,0:T(8,128)(2,1)}), bf16[1536,1536]{1,0:T(8,128)(2,1)}) %all-gather.3.cloned.1.call-update) | async-done | bytes 4718608 | tf_op jit(solution)/shard_map/all_gather | solution.py:64
  136.1 54.3 %all-gather.5.cloned.1.call-done = bf16[1536,1536]{1,0:T(8,128)(2,1)} async-done(((bf16[96,1536]{1,0:T(8,128)(2,1)}), bf16[1536,1536]{1,0:T(8,128)(2,1)}) %all-gather.5.cloned.1.call-update) | async-done | bytes 4718608 | tf_op jit(solution)/shard_map/all_gather | solution.py:65
  190.4 109.9 %while.18 = (s32[]{:T(128)}, f32[24,384]{1,0:T(8,128)S(1)}, f32[24,384]{1,0:T(8,128)S(1)}, f32[24,384,64]{1,2,0:T(8,128)}, bf16[1536,1536]{1,0:T(8,128)(2,1)}, /...) while((s32[]{:T(128)}, f32[24,384]{1,0:T(8,128)S(1)}, ...), condition=%wide.region_11.14_spmd.clone, body=%wide.region_8.13_spmd.clone.sunk | while | flops 1247523840 | bytes 78839976 | solution.py:93
  190.4 3.9 %constant_dynamic-slice_fusion.3 = (bf16[512,1536]{1,0:T(8,128)(2,1)}, bf16[512,1536]{1,0:T(8,128)(2,1)}) fusion(bf16[1536,1536]{1,0:T(8,128)(2,1)} %get-tuple-element.309, s32[]{:T(128)S(6)} %select_n.64, bf16[1536,1536]{1,0:T(8,128)(2,1)} %get-tuple-element.307), kind=kLoop, calls=%fused_computation.18.clone.1 | loop fusion | bytes 6291460 | tf_op jit(solution)/shard_map/while/body/eval_jaxpr/dynamic_slice | solution.py:74
  196.0 7.9 %bitcast_reduce_fusion.2 = (f32[24,384]{1,0:T(8,128)S(1)}, f32[24,512,384]{2,1,0:T(8,128)}) fusion(bf16[512,24,64]{0,2,1:T(8,128)(2,1)S(1)} %bitcast.55, bf16[384,24,64]{0,2,1:T(8,128)(2,1)S(1)} %get-tuple-element.308), kind=kOutput, calls=%fused_computation.5.clone.1 | convolution fusion | flops 613407744 | bytes 21663744 | tf_op jit(solution)/shard_map/while/body/eval_jaxpr/qhd,khd->hqk/dot_general | solution.py:78
  203.9 9.5 %fusion.32 = f32[24,384]{1,0:T(8,128)S(1)} fusion(f32[24,512,384]{2,1,0:T(8,128)} %get-tuple-element.277, f32[24,384]{1,0:T(8,128)S(1)} %select_maximum_fusion.2), kind=kLoop, calls=%fused_computation.8.clone.1 | loop fusion | flops 14146560 | bytes 18948096 | tf_op jit(solution)/shard_map/while/body/eval_jaxpr/reduce_sum | solution.py:84
  213.4 1.7 copy.48
  215.1 11.4 %fusion.34 = f32[24,384,64]{1,2,0:T(8,128)} fusion(f32[24,384,64]{1,2,0:T(8,128)} %get-tuple-element.295, bf16[512,24,64]{0,2,1:T(8,128)(2,1)S(1)} %bitcast.54, f32[24,512,384]{2,1,0:T(8,128)} %get-tuple-element.277, f32[24,384]{1,0:T(8,128)S(1)} %select_maximum_fusion.2, f32[24,384]{1,0:T(8,128)S(1)} %get-tuple-element.280, pred[]{:T(512)S(6)} %compare.3), kind=kOutput, calls=%fused_computation.13.clone.1 | convolution fusion | flops 619905024 | bytes 25239552 | tf_op jit(solution)/shard_map/while/body/eval_jaxpr/hqk,khd->hqd/dot_general | solution.py:85
  226.6 3.9 %constant_dynamic-slice_fusion.3 = (bf16[512,1536]{1,0:T(8,128)(2,1)}, bf16[512,1536]{1,0:T(8,128)(2,1)}) fusion(bf16[1536,1536]{1,0:T(8,128)(2,1)} %get-tuple-element.309, s32[]{:T(128)S(6)} %select_n.64, bf16[1536,1536]{1,0:T(8,128)(2,1)} %get-tuple-element.307), kind=kLoop, calls=%fused_computation.18.clone.1 | loop fusion | bytes 6291460 | tf_op jit(solution)/shard_map/while/body/eval_jaxpr/dynamic_slice | solution.py:74
  232.2 7.9 %bitcast_reduce_fusion.2 = (f32[24,384]{1,0:T(8,128)S(1)}, f32[24,512,384]{2,1,0:T(8,128)}) fusion(bf16[512,24,64]{0,2,1:T(8,128)(2,1)S(1)} %bitcast.55, bf16[384,24,64]{0,2,1:T(8,128)(2,1)S(1)} %get-tuple-element.308), kind=kOutput, calls=%fused_computation.5.clone.1 | convolution fusion | flops 613407744 | bytes 21663744 | tf_op jit(solution)/shard_map/while/body/eval_jaxpr/qhd,khd->hqk/dot_general | solution.py:78
  240.1 9.5 %fusion.32 = f32[24,384]{1,0:T(8,128)S(1)} fusion(f32[24,512,384]{2,1,0:T(8,128)} %get-tuple-element.277, f32[24,384]{1,0:T(8,128)S(1)} %select_maximum_fusion.2), kind=kLoop, calls=%fused_computation.8.clone.1 | loop fusion | flops 14146560 | bytes 18948096 | tf_op jit(solution)/shard_map/while/body/eval_jaxpr/reduce_sum | solution.py:84
  249.6 1.7 copy.48
  251.3 12.1 %fusion.34 = f32[24,384,64]{1,2,0:T(8,128)} fusion(f32[24,384,64]{1,2,0:T(8,128)} %get-tuple-element.295, bf16[512,24,64]{0,2,1:T(8,128)(2,1)S(1)} %bitcast.54, f32[24,512,384]{2,1,0:T(8,128)} %get-tuple-element.277, f32[24,384]{1,0:T(8,128)S(1)} %select_maximum_fusion.2, f32[24,384]{1,0:T(8,128)S(1)} %get-tuple-element.280, pred[]{:T(512)S(6)} %compare.3), kind=kOutput, calls=%fused_computation.13.clone.1 | convolution fusion | flops 619905024 | bytes 25239552 | tf_op jit(solution)/shard_map/while/body/eval_jaxpr/hqk,khd->hqd/dot_general | solution.py:85
  263.4 3.9 %constant_dynamic-slice_fusion.3 = (bf16[512,1536]{1,0:T(8,128)(2,1)}, bf16[512,1536]{1,0:T(8,128)(2,1)}) fusion(bf16[1536,1536]{1,0:T(8,128)(2,1)} %get-tuple-element.309, s32[]{:T(128)S(6)} %select_n.64, bf16[1536,1536]{1,0:T(8,128)(2,1)} %get-tuple-element.307), kind=kLoop, calls=%fused_computation.18.clone.1 | loop fusion | bytes 6291460 | tf_op jit(solution)/shard_map/while/body/eval_jaxpr/dynamic_slice | solution.py:74
  269.0 7.9 %bitcast_reduce_fusion.2 = (f32[24,384]{1,0:T(8,128)S(1)}, f32[24,512,384]{2,1,0:T(8,128)}) fusion(bf16[512,24,64]{0,2,1:T(8,128)(2,1)S(1)} %bitcast.55, bf16[384,24,64]{0,2,1:T(8,128)(2,1)S(1)} %get-tuple-element.308), kind=kOutput, calls=%fused_computation.5.clone.1 | convolution fusion | flops 613407744 | bytes 21663744 | tf_op jit(solution)/shard_map/while/body/eval_jaxpr/qhd,khd->hqk/dot_general | solution.py:78
  277.0 9.5 %fusion.32 = f32[24,384]{1,0:T(8,128)S(1)} fusion(f32[24,512,384]{2,1,0:T(8,128)} %get-tuple-element.277, f32[24,384]{1,0:T(8,128)S(1)} %select_maximum_fusion.2), kind=kLoop, calls=%fused_computation.8.clone.1 | loop fusion | flops 14146560 | bytes 18948096 | tf_op jit(solution)/shard_map/while/body/eval_jaxpr/reduce_sum | solution.py:84
  286.5 1.7 copy.48
  288.2 12.1 %fusion.34 = f32[24,384,64]{1,2,0:T(8,128)} fusion(f32[24,384,64]{1,2,0:T(8,128)} %get-tuple-element.295, bf16[512,24,64]{0,2,1:T(8,128)(2,1)S(1)} %bitcast.54, f32[24,512,384]{2,1,0:T(8,128)} %get-tuple-element.277, f32[24,384]{1,0:T(8,128)S(1)} %select_maximum_fusion.2, f32[24,384]{1,0:T(8,128)S(1)} %get-tuple-element.280, pred[]{:T(512)S(6)} %compare.3), kind=kOutput, calls=%fused_computation.13.clone.1 | convolution fusion | flops 619905024 | bytes 25239552 | tf_op jit(solution)/shard_map/while/body/eval_jaxpr/hqk,khd->hqd/dot_general | solution.py:85
  300.3 2.1 divide_convert_fusion
  302.7 9.1 %add_convert_fusion = bf16[384,3072]{1,0:T(8,128)(2,1)} fusion(bf16[384,3072]{1,0:T(8,128)(2,1)S(1)} %copy-done.5, bf16[384,1536]{0,1:T(8,128)(2,1)S(1)} %bitcast.62, bf16[1536,3072]{1,0:T(8,128)(2,1)} %param.16, bf16[384]{0:T(512)(128)(2,1)S(1)} %broadcast_bitcast_fusion), kind=kOutput, calls=%fused_computation.21 | convolution fusion | flops 3630956544 | bytes 15336192 | tf_op jit(solution)/shard_map/dot_general | solution.py:118
  (65 shorter events, 19.3 us)
Async XLA Ops:
  6.5 2.6 copy-start
  6.5 3.3 %copy-start.2 = (bf16[384,1536]{1,0:T(8,128)(2,1)S(1)}, bf16[384,1536]{1,0:T(8,128)(2,1)}, u32[]{:S(2)}) copy-start(bf16[384,1536]{1,0:T(8,128)(2,1)} %param.15) | copy-start | bytes 3538948
  12.4 32.5 %all-to-all-start = ((bf16[24,16,1536]{2,0,1:T(8,128)(2,1)}), bf16[24,16,1536]{2,0,1:T(8,128)(2,1)S(1)}, u32[]{:S(2)}, u32[]{:S(2)}) async-start(bf16[24,16,1536]{2,0,1:T(8,128)(2,1)} %copy.35), calls=%async_computation | async-start | bytes 2359296 | tf_op jit(solution)/shard_map/all_to_all | solution.py:111
  19.8 32.7 %copy-start.6 = (s32[12]{0:T(128)S(1)}, s32[12]{0:T(128)}, u32[]{:S(2)}) copy-start(s32[12]{0:T(128)} %param.17) | copy-start | bytes 148
  44.9 32.6 %all-to-all-start.1 = ((bf16[24,16,1536]{2,0,1:T(8,128)(2,1)}), bf16[24,16,1536]{2,0,1:T(8,128)(2,1)S(1)}, u32[]{:S(2)}, u32[]{:S(2)}) async-start(bf16[24,16,1536]{2,0,1:T(8,128)(2,1)} %copy.38), calls=%async_computation.1 | async-start | bytes 2359296 | tf_op jit(solution)/shard_map/all_to_all | solution.py:112
  52.4 83.7 %all-gather.3.cloned.1.call-start = ((), (), s32[]{:S(2)}) async-start(), calls=%async_computation.2 | async-start | bytes 5013504 | tf_op jit(solution)/shard_map/all_gather | solution.py:64
  77.9 1.0 copy-start.4
  77.9 2.7 copy-start.3
  79.8 110.6 %all-gather.5.cloned.1.call-start = ((), (), s32[]{:S(2)}) async-start(), calls=%async_computation.3 | async-start | bytes 5013504 | tf_op jit(solution)/shard_map/all_gather | solution.py:65
  300.3 2.4 copy-start.5
  302.7 9.1 %copy-start.1 = (bf16[384,1536]{1,0:T(8,128)(2,1)S(1)}, bf16[384,1536]{1,0:T(8,128)(2,1)}, u32[]{:S(2)}) copy-start(bf16[384,1536]{1,0:T(8,128)(2,1)} %param.14) | copy-start | bytes 3538948
Sparse Core Ops, SparseCore 0:
  79.9 56.1 all-gather.2
  138.4 51.9 all-gather.4
where the time goes:
time: 319 us
  waiting for transfers between devices  156 us (49%)
  matrix products  68.5 us (21%)
  other arithmetic  34.9 us (11%)
  local copies, waits for them, and re-layouts  30.8 us (10%)
  starting transfers between devices  15.1 us (5%)
  between operations  13.6 us (4%)
    all_gather x1, waiting for transfers between devices, attend(): key_piece = lax.all_gather(keys_own, 'seq', axis=0, tiled=True)  54.7 us
    all_gather x1, waiting for transfers between devices, attend(): value_piece = lax.all_gather(values_own, 'seq', axis=0, tiled=True)  54.3 us
    dot_general x3, matrix products, one_block(): jnp.einsum('hqk,khd->hqd', weights.astype(jnp.bfloat16), value_block, pre...  35.6 us
    reduce_sum x3, other arithmetic, one_block(): total = total * fade + jnp.sum(weights, axis=2)  28.4 us
    dot_general x3, matrix products, one_block(): jnp.einsum('qhd,khd->hqk', query_grid, key_block, preferred_element_type=...  23.8 us
    all_to_all x1, waiting for transfers between devices, body(): lax.all_to_all(sent[0], 'seq', split_axis=1, concat_axis=1, tiled=True)  23.5 us
    all_to_all x1, waiting for transfers between devices, body(): lax.all_to_all(sent[1], 'seq', split_axis=1, concat_axis=1, tiled=True)  22.6 us
    dynamic_slice x6, local copies, waits for them, and re-layouts, one_block(): lax.dynamic_slice_in_dim(value_piece, index_block * block, block, 0)  16.7 us
  transfers between devices with their start and end apart: 4, of which 4 were waited for; matrix products, arithmetic and copies ran while one was open for 2% of the time, Pallas kernels for 0%

commit v1 on v0

v1 whole, which is shorter than its diff:
```python
import functools
import math

import jax
import jax.numpy as jnp
from jax import lax
from jax.experimental import pallas as pl
from jax.experimental.pallas import tpu as pltpu
from jax.sharding import PartitionSpec as P

HEADS = 24
TILE = 128
TILES_DEV = 3
LANES = 128
MESH = pl.DeviceIdType.MESH


def ring_device(place, chips, core):
    place = lax.rem(place + chips, chips)
    if chips == 8:
        chip = jnp.where(place < 4, 2 * place, 2 * (7 - place) + 1)
    else:
        chip = place
    return 2 * chip + core


def ring_place(device, chips):
    chip = device // 2
    if chips == 8:
        return jnp.where(lax.rem(chip, 2) == 0, chip // 2, 7 - chip // 2)
    return chip


def attend_kernel(n, own_ref, q_ref, o_ref, kv, qs, best, acc, hop_send, hop_recv, mate_send, mate_recv):
    device = lax.axis_index("seq")
    core = lax.rem(device, 2)
    chips = n // 2
    half = chips // 2
    place = ring_place(device, chips)
    sides = (ring_device(place + 1, chips, core), ring_device(place - 1, chips, core))
    mate = device + 1 - 2 * core
    rows = own_ref.shape[0]
    width = q_ref.shape[1]
    pairs = width // LANES

    barrier = pltpu.get_barrier_semaphore()
    for other in (*sides, mate):
        pl.semaphore_signal(barrier, inc=1, device_id={"seq": other}, device_id_type=MESH)
    pl.semaphore_wait(barrier, 3)

    def slot(step):
        return 0 if step == 0 else 2 * rows + (step - 1) * 4 * rows

    def region(step, side, start=0, size=rows):
        base = slot(step) + (2 * rows * side if step < half else 0) + start
        return pl.ds(pl.multiple_of(base + core * rows, 16), size)

    def hop(src, dst, step, side):
        copy = pltpu.make_async_remote_copy(
            src_ref=src, dst_ref=kv.at[dst], send_sem=hop_send.at[side, step], recv_sem=hop_recv.at[side, step],
            device_id={"seq": sides[side]}, device_id_type=MESH)
        copy.start()
        return copy

    def share(src, dst, step, side):
        copy = pltpu.make_async_remote_copy(
            src_ref=src, dst_ref=kv.at[dst], send_sem=mate_send.at[side, step], recv_sem=mate_recv.at[side, step],
            device_id={"seq": mate}, device_id_type=MESH)
        copy.start()
        return copy

    def compute(start, length, first):
        def one_pair(h, carry):
            columns = pl.ds(pl.multiple_of(h * LANES, LANES), LANES)
            value_columns = pl.ds(pl.multiple_of(width + h * LANES, LANES), LANES)
            keys = kv[start:start + length, columns]
            values = kv[start:start + length, value_columns]
            low = lax.broadcasted_iota(jnp.int32, (1, LANES), 1) < LANES // 2
            for odd in range(2):
                mine = low if odd == 0 else jnp.logical_not(low)
                value_one = jnp.where(mine, values, jnp.ones_like(values))
                scores = lax.dot_general(qs[h, odd], keys, (((1,), (1,)), ((), ())), preferred_element_type=jnp.float32)
                top = jnp.max(scores, axis=1, keepdims=True)
                if first:
                    weights = jnp.exp(scores - top)
                    acc[h, odd] = jnp.dot(weights.astype(jnp.bfloat16), value_one, preferred_element_type=jnp.float32)
                    best[h, odd] = top
                else:
                    old = best[h, odd]
                    new = jnp.maximum(old, top)
                    weights = jnp.exp(scores - new)
                    part = jnp.dot(weights.astype(jnp.bfloat16), value_one, preferred_element_type=jnp.float32)
                    acc[h, odd] = acc[h, odd] * jnp.exp(old - new) + part
                    best[h, odd] = new
            return carry

        lax.fori_loop(0, pairs, one_pair, 0)

    sent = []
    hops = [hop(own_ref, region(1, side), 1, side) for side in range(2)]
    mates = [share(own_ref, region(0, 0), 0, 0)]
    sent += hops + mates
    kv[region(0, 0), :] = own_ref[...]

    scale = 1.0 / math.sqrt(width // HEADS)

    def split_pair(h, carry):
        columns = pl.ds(pl.multiple_of(h * LANES, LANES), LANES)
        both = q_ref[:, columns].astype(jnp.float32) * scale
        low = lax.broadcasted_iota(jnp.int32, (1, LANES), 1) < LANES // 2
        qs[h, 0] = jnp.where(low, both, 0.0).astype(jnp.bfloat16)
        qs[h, 1] = jnp.where(low, 0.0, both).astype(jnp.bfloat16)
        return carry

    lax.fori_loop(0, pairs, split_pair, 0)

    for step in range(1, half + 1):
        for copy in hops:
            copy.wait_recv()
        new_mates = []
        if step < half:
            if step < half - 1:
                hops = [hop(kv.at[region(step, side)], region(step + 1, side), step + 1, side) for side in range(2)]
            else:
                hops = [
                    hop(kv.at[region(step, side, side * rows // 2, rows // 2)],
                        region(step + 1, side, side * rows // 2, rows // 2), step + 1, side)
                    for side in range(2)
                ]
            sent += hops
            new_mates = [share(kv.at[region(step, side)], region(step, side), step, side) for side in range(2)]
        else:
            new_mates = [share(kv.at[region(step, 0)], region(step, 0), step, 0)]
        sent += new_mates
        for copy in mates:
            copy.wait_recv()
        mates = new_mates
        compute(slot(step - 1), slot(step) - slot(step - 1), step == 1)
    for copy in mates:
        copy.wait_recv()
    compute(slot(half), 2 * rows, False)

    def finish(h, carry):
        columns = pl.ds(pl.multiple_of(h * LANES, LANES), LANES)
        low = lax.broadcasted_iota(jnp.int32, (1, LANES), 1) < LANES // 2
        even, odd = acc[h, 0], acc[h, 1]
        total_even = even[:, LANES // 2:LANES // 2 + 1]
        total_odd = odd[:, 0:1]
        o_ref[:, columns] = jnp.where(low, even / total_even, odd / total_odd).astype(jnp.bfloat16)
        return carry

    lax.fori_loop(0, pairs, finish, 0)
    for copy in sent:
        copy.wait_send()


def attend(own, queries, n):
    rows, width = queries.shape
    pairs = width // LANES
    half = n // 4
    vmem = pl.BlockSpec(memory_space=pltpu.VMEM)
    return pl.pallas_call(
        functools.partial(attend_kernel, n),
        out_shape=jax.ShapeDtypeStruct((rows, width), jnp.bfloat16),
        in_specs=[vmem, vmem],
        out_specs=vmem,
        scratch_shapes=[
            pltpu.VMEM((own.shape[0] * n, 2 * width), jnp.bfloat16),
            pltpu.VMEM((pairs, 2, rows, LANES), jnp.bfloat16),
            pltpu.VMEM((pairs, 2, rows, 1), jnp.float32),
            pltpu.VMEM((pairs, 2, rows, LANES), jnp.float32),
            pltpu.SemaphoreType.DMA((2, half + 1)),
            pltpu.SemaphoreType.DMA((2, half + 1)),
            pltpu.SemaphoreType.DMA((2, half + 1)),
            pltpu.SemaphoreType.DMA((2, half + 1)),
        ],
        compiler_params=pltpu.CompilerParams(
            collective_id=0, has_side_effects=True, vmem_limit_bytes=52 * 1024 * 1024
        ),
    )(own, queries)


def body(hidden, query_rows, key_rows, value_rows, out_weight, masked_tiles):
    n = lax.axis_size("seq")
    device = lax.axis_index("seq")
    tokens, width = key_rows.shape
    both = jnp.concatenate([key_rows, value_rows], axis=1).reshape(TILES_DEV, TILE, 2 * width)
    got = lax.all_to_all(both, "seq", split_axis=1, concat_axis=0, tiled=True)
    own = jnp.take(got, masked_tiles, axis=0, mode="clip").reshape(-1, 2 * width)
    attended = attend(own, query_rows, n)
    here = device * TILES_DEV + jnp.arange(tokens, dtype=jnp.int32) // TILE
    masked = jnp.any(here[:, None] == masked_tiles[None, :], axis=1)
    residual = jnp.dot(attended, out_weight, preferred_element_type=jnp.float32).astype(jnp.bfloat16)
    residual = jnp.where(masked[:, None], residual, jnp.zeros_like(residual))
    painted = hidden.astype(jnp.float32) + residual.astype(jnp.float32)
    return painted.astype(jnp.bfloat16)


def solution(mesh):
    placed = (
        P(("groups", "seq"), None),
        P(("groups", "seq"), None),
        P(("groups", "seq"), None),
        P(("groups", "seq"), None),
        P(),
        P("groups"),
    )
    return jax.shard_map(
        body, mesh=mesh, in_specs=placed, out_specs=P(("groups", "seq"), None), check_vma=False
    )
```

time: 319 us -> 190 us (0.60)
  Pallas kernels: 0 us -> 106 us
  waiting for transfers between devices: 156 us -> 59.2 us
  matrix products: 68.5 us -> 8.81 us
  other arithmetic: 34.9 us -> 1.97 us
  local copies, waits for them, and re-layouts: 30.8 us -> 5.32 us
  between operations: 13.6 us -> 0.09 us
  starting transfers between devices: 15.1 us -> 7.52 us
    all_gather x2 -> x0, waiting for transfers between devices: 109 us -> none  [the longest x1 54.7 us: attend(): key_piece = lax.all_gather(keys_own, 'seq', axis=0, tiled=True)]
    pallas_call x0 -> x1, Pallas kernels: none -> 106 us  [attend(): pl.pallas_call(functools.partial(attend_kernel, n), out_shape=jax.ShapeDt...]
    dot_general x6 -> x0, matrix products: 59.4 us -> none  [the longest x3 35.6 us: one_block(): jnp.einsum('hqk,khd->hqd', weights.astype(jnp.bfloat16), value_block, pre...]
    reduce_sum x8 -> x0, other arithmetic: 29.5 us -> none  [the longest x3 28.4 us: one_block(): total = total * fade + jnp.sum(weights, axis=2)]
    dynamic_slice x9 -> x0, local copies, waits for them, and re-layouts: 21.9 us -> none  [the longest x6 16.7 us: one_block(): lax.dynamic_slice_in_dim(value_piece, index_block * block, block, 0)]
    all_to_all x2 -> x1, waiting for transfers between devices: 46.1 us -> 59.2 us  [body(): got = lax.all_to_all(both, 'seq', split_axis=1, concat_axis=0, tiled=True)]
    all_to_all x2 -> x1, starting transfers between devices: 14.9 us -> 7.52 us  [body(): got = lax.all_to_all(both, 'seq', split_axis=1, concat_axis=0, tiled=True)]
  transfers between devices with their start and end apart: 4 -> 1, of which waited for: 4 -> 1; matrix products, arithmetic and copies ran while one was open for 2% -> 0% of each run, Pallas kernels for 0% -> 0%
where the time goes in v1:
time: 190 us; the launch traced here: 189 us
  Pallas kernels  106 us (56%)
  waiting for transfers between devices  59.2 us (31%)
  matrix products  8.81 us (5%)
  starting transfers between devices  7.52 us (4%)
  local copies, waits for them, and re-layouts  5.32 us (3%)
  other arithmetic  1.97 us (1%)
    pallas_call x1, Pallas kernels, attend(): pl.pallas_call(functools.partial(attend_kernel, n), out_shape=jax.ShapeDt...  106 us
    all_to_all x1, waiting for transfers between devices, body(): got = lax.all_to_all(both, 'seq', split_axis=1, concat_axis=0, tiled=True)  59.2 us
    dot_general x1, matrix products, body(): jnp.dot(attended, out_weight, preferred_element_type=jnp.float32)  8.81 us
    all_to_all x1, starting transfers between devices, body(): got = lax.all_to_all(both, 'seq', split_axis=1, concat_axis=0, tiled=True)  7.52 us
  transfers between devices with their start and end apart: 1, of which 1 were waited for; matrix products, arithmetic and copies ran while one was open for 0% of the time, Pallas kernels for 0%

profile of v1, /device:TPU:0, one launch (start us, length us, event | category | flops | bytes accessed | tf_op | source)
XLA Modules:
  0.0 189.4 jit_solution(16493310266309699232)
XLA Ops:
  0.0 1.9 pad_maximum_fusion
  1.9 3.7 %copy.13 = bf16[3,128,3072]{2,0,1:T(4,128)(2,1)} copy(bf16[3,128,3072]{2,1,0:T(8,128)(2,1)S(1)} %bitcast.12) | data formatting | bytes 4718592 | tf_op jit(solution)/shard_map/reshape | solution.py:187
  5.6 0.0 copy-start
  5.6 7.5 %all-to-all-start = ((bf16[3,128,3072]{2,0,1:T(4,128)(2,1)}), bf16[3,128,3072]{2,0,1:T(4,128)(2,1)S(1)}, u32[]{:S(2)}, u32[]{:S(2)}) async-start(bf16[3,128,3072]{2,0,1:T(4,128)(2,1)} %copy.13), calls=%async_computation | async-start | bytes 6291456 | tf_op jit(solution)/shard_map/all_to_all | solution.py:188
  13.1 0.0 copy-done
  13.1 0.1 compare_reduce_fusion
  13.2 59.2 %all-to-all-done = bf16[3,128,3072]{2,0,1:T(4,128)(2,1)S(1)} async-done(((bf16[3,128,3072]{2,0,1:T(4,128)(2,1)}), bf16[3,128,3072]{2,0,1:T(4,128)(2,1)S(1)}, u32[]{:S(2)}, u32[]{:S(2)}) %all-to-all-start) | async-done | bytes 2359328 | tf_op jit(solution)/shard_map/all_to_all | solution.py:188
  72.4 0.9 copy.17
  73.3 0.2 copy.15
  73.5 0.6 gather_fusion
  74.1 0.0 copy-start.1
  74.1 106.5 %shard_map.64 = bf16[384,1536]{1,0:T(8,128)(2,1)S(1)} custom-call(bf16[96,3072]{1,0:T(8,128)(2,1)S(1)} %bitcast.10, bf16[384,1536]{1,0:T(8,128)(2,1)} %q_ref.1), custom_call_target="tpu_custom_call" | custom-call | tf_op jit(solution)/shard_map/pallas_call | solution.py:162
  180.6 0.0 copy-done.1
  180.6 8.8 %add_convert_fusion = bf16[384,3072]{1,0:T(8,128)(2,1)} fusion(bf16[384,3072]{1,0:T(8,128)(2,1)S(1)} %copy-done.1, bf16[384,1536]{1,0:T(8,128)(2,1)S(1)} %shard_map.64, bf16[1536,3072]{1,0:T(8,128)(2,1)} %param.10, pred[384]{0:T(512)(128)(4,1)S(1)} %compare_reduce_fusion), kind=kOutput, calls=%fused_computation.1 | convolution fusion | flops 3630956544 | bytes 15335808 | tf_op jit(solution)/shard_map/dot_general | solution.py:193
  (2 shorter events, 0.0 us)
Async XLA Ops:
  5.6 7.5 %copy-start = (s32[12]{0:T(128)S(1)}, s32[12]{0:T(128)}, u32[]{:S(2)}) copy-start(s32[12]{0:T(128)} %param.11) | copy-start | bytes 148
  5.6 66.9 %all-to-all-start = ((bf16[3,128,3072]{2,0,1:T(4,128)(2,1)}), bf16[3,128,3072]{2,0,1:T(4,128)(2,1)S(1)}, u32[]{:S(2)}, u32[]{:S(2)}) async-start(bf16[3,128,3072]{2,0,1:T(4,128)(2,1)} %copy.13), calls=%async_computation | async-start | bytes 6291456 | tf_op jit(solution)/shard_map/all_to_all | solution.py:188
  74.1 106.5 %copy-start.1 = (bf16[384,3072]{1,0:T(8,128)(2,1)S(1)}, bf16[384,3072]{1,0:T(8,128)(2,1)}, u32[]{:S(2)}) copy-start(bf16[384,3072]{1,0:T(8,128)(2,1)} %param.6) | copy-start | bytes 7077892

commit v2 on v1

--- a/solution.py
+++ b/solution.py
@@ -12,6 +12,8 @@
 TILE = 128
 TILES_DEV = 3
 LANES = 128
+HALF = 64
+ONES = 16
 MESH = pl.DeviceIdType.MESH
 
 
@@ -40,7 +42,7 @@
     sides = (ring_device(place + 1, chips, core), ring_device(place - 1, chips, core))
     mate = device + 1 - 2 * core
     rows = own_ref.shape[0]
-    width = q_ref.shape[1]
+    queries, width = q_ref.shape
     pairs = width // LANES
 
     barrier = pltpu.get_barrier_semaphore()
@@ -74,27 +76,28 @@
             columns = pl.ds(pl.multiple_of(h * LANES, LANES), LANES)
             value_columns = pl.ds(pl.multiple_of(width + h * LANES, LANES), LANES)
             keys = kv[start:start + length, columns]
-            values = kv[start:start + length, value_columns]
-            low = lax.broadcasted_iota(jnp.int32, (1, LANES), 1) < LANES // 2
+            values = jnp.transpose(kv[start:start + length, value_columns])
+            ones = jnp.ones((ONES, length), jnp.bfloat16)
+            both = jnp.dot(keys, qs[h], preferred_element_type=jnp.float32)
             for odd in range(2):
-                mine = low if odd == 0 else jnp.logical_not(low)
-                value_one = jnp.where(mine, values, jnp.ones_like(values))
-                scores = lax.dot_general(qs[h, odd], keys, (((1,), (1,)), ((), ())), preferred_element_type=jnp.float32)
-                top = jnp.max(scores, axis=1, keepdims=True)
+                mine = values[odd * HALF:(odd + 1) * HALF]
+                value_one = jnp.concatenate([mine, ones], axis=0)
+                scores = both[:, odd * queries:(odd + 1) * queries]
+                top = jnp.max(scores, axis=0, keepdims=True)
                 if first:
                     weights = jnp.exp(scores - top)
-                    acc[h, odd] = jnp.dot(weights.astype(jnp.bfloat16), value_one, preferred_element_type=jnp.float32)
+                    acc[h, odd] = jnp.dot(value_one, weights.astype(jnp.bfloat16), preferred_element_type=jnp.float32)
                     best[h, odd] = top
                 else:
                     old = best[h, odd]
                     new = jnp.maximum(old, top)
                     weights = jnp.exp(scores - new)
-                    part = jnp.dot(weights.astype(jnp.bfloat16), value_one, preferred_element_type=jnp.float32)
+                    part = jnp.dot(value_one, weights.astype(jnp.bfloat16), preferred_element_type=jnp.float32)
                     acc[h, odd] = acc[h, odd] * jnp.exp(old - new) + part
                     best[h, odd] = new
             return carry
 
-        lax.fori_loop(0, pairs, one_pair, 0)
+        lax.fori_loop(0, pairs, one_pair, 0, unroll=2)
 
     sent = []
     hops = [hop(own_ref, region(1, side), 1, side) for side in range(2)]
@@ -106,10 +109,10 @@
 
     def split_pair(h, carry):
         columns = pl.ds(pl.multiple_of(h * LANES, LANES), LANES)
-        both = q_ref[:, columns].astype(jnp.float32) * scale
-        low = lax.broadcasted_iota(jnp.int32, (1, LANES), 1) < LANES // 2
-        qs[h, 0] = jnp.where(low, both, 0.0).astype(jnp.bfloat16)
-        qs[h, 1] = jnp.where(low, 0.0, both).astype(jnp.bfloat16)
+        both = jnp.transpose(q_ref[:, columns].astype(jnp.float32) * scale)
+        low = lax.broadcasted_iota(jnp.int32, (LANES, 1), 0) < HALF
+        qs[h, :, :queries] = jnp.where(low, both, 0.0).astype(jnp.bfloat16)
+        qs[h, :, queries:] = jnp.where(low, 0.0, both).astype(jnp.bfloat16)
         return carry
 
     lax.fori_loop(0, pairs, split_pair, 0)
@@ -142,11 +145,8 @@
 
     def finish(h, carry):
         columns = pl.ds(pl.multiple_of(h * LANES, LANES), LANES)
-        low = lax.broadcasted_iota(jnp.int32, (1, LANES), 1) < LANES // 2
-        even, odd = acc[h, 0], acc[h, 1]
-        total_even = even[:, LANES // 2:LANES // 2 + 1]
-        total_odd = odd[:, 0:1]
-        o_ref[:, columns] = jnp.where(low, even / total_even, odd / total_odd).astype(jnp.bfloat16)
+        done = [acc[h, odd, :HALF] / acc[h, odd, HALF:HALF + 1] for odd in range(2)]
+        o_ref[:, columns] = jnp.transpose(jnp.concatenate(done, axis=0)).astype(jnp.bfloat16)
         return carry
 
     lax.fori_loop(0, pairs, finish, 0)
@@ -166,9 +166,9 @@
         out_specs=vmem,
         scratch_shapes=[
             pltpu.VMEM((own.shape[0] * n, 2 * width), jnp.bfloat16),
-            pltpu.VMEM((pairs, 2, rows, LANES), jnp.bfloat16),
-            pltpu.VMEM((pairs, 2, rows, 1), jnp.float32),
-            pltpu.VMEM((pairs, 2, rows, LANES), jnp.float32),
+            pltpu.VMEM((pairs, LANES, 2 * rows), jnp.bfloat16),
+            pltpu.VMEM((pairs, 2, 1, rows), jnp.float32),
+            pltpu.VMEM((pairs, 2, HALF + ONES, rows), jnp.float32),
             pltpu.SemaphoreType.DMA((2, half + 1)),
             pltpu.SemaphoreType.DMA((2, half + 1)),
             pltpu.SemaphoreType.DMA((2, half + 1)),

time: 190 us -> 160 us (0.84)
  Pallas kernels: 106 us -> 76.9 us
    pallas_call x1, Pallas kernels: 106 us -> 76.9 us  [attend(): pl.pallas_call(functools.partial(attend_kernel, n), out_shape=jax.ShapeDt...]
where the time goes in v2:
time: 160 us
  Pallas kernels  76.9 us (48%)
  waiting for transfers between devices  59.2 us (37%)
  matrix products  8.81 us (6%)
  starting transfers between devices  7.52 us (5%)
  local copies, waits for them, and re-layouts  5.32 us (3%)
  other arithmetic  1.97 us (1%)
    pallas_call x1, Pallas kernels, attend(): pl.pallas_call(functools.partial(attend_kernel, n), out_shape=jax.ShapeDt...  76.9 us
    all_to_all x1, waiting for transfers between devices, body(): got = lax.all_to_all(both, 'seq', split_axis=1, concat_axis=0, tiled=True)  59.2 us
    dot_general x1, matrix products, body(): jnp.dot(attended, out_weight, preferred_element_type=jnp.float32)  8.81 us
    all_to_all x1, starting transfers between devices, body(): got = lax.all_to_all(both, 'seq', split_axis=1, concat_axis=0, tiled=True)  7.52 us
    reshape x1, local copies, waits for them, and re-layouts, body(): jnp.concatenate([key_rows, value_rows], axis=1)  3.68 us
  transfers between devices with their start and end apart: 1, of which 1 were waited for; matrix products, arithmetic and copies ran while one was open for 0% of the time, Pallas kernels for 0%

profile of v2, /device:TPU:0, one launch (start us, length us, event | category | flops | bytes accessed | tf_op | source)
XLA Modules:
  0.0 159.8 jit_solution(15675587302636474047)
XLA Ops:
  0.0 1.9 %pad_maximum_fusion = bf16[384,3072]{1,0:T(8,128)(2,1)S(1)} fusion(bf16[384,1536]{1,0:T(8,128)(2,1)} %param.9, bf16[384,1536]{1,0:T(8,128)(2,1)} %param.8), kind=kLoop, calls=%fused_computation.4 | loop fusion | flops 4718592 | bytes 4718592 | tf_op jit(solution)/shard_map/concatenate | solution.py:187
  1.9 3.7 %copy.13 = bf16[3,128,3072]{2,0,1:T(4,128)(2,1)} copy(bf16[3,128,3072]{2,1,0:T(8,128)(2,1)S(1)} %bitcast.12) | data formatting | bytes 4718592 | tf_op jit(solution)/shard_map/reshape | solution.py:187
  5.6 0.0 copy-start
  5.6 7.5 %all-to-all-start = ((bf16[3,128,3072]{2,0,1:T(4,128)(2,1)}), bf16[3,128,3072]{2,0,1:T(4,128)(2,1)S(1)}, u32[]{:S(2)}, u32[]{:S(2)}) async-start(bf16[3,128,3072]{2,0,1:T(4,128)(2,1)} %copy.13), calls=%async_computation | async-start | bytes 6291456 | tf_op jit(solution)/shard_map/all_to_all | solution.py:188
  13.1 0.0 copy-done
  13.1 0.1 compare_reduce_fusion
  13.2 59.2 %all-to-all-done = bf16[3,128,3072]{2,0,1:T(4,128)(2,1)S(1)} async-done(((bf16[3,128,3072]{2,0,1:T(4,128)(2,1)}), bf16[3,128,3072]{2,0,1:T(4,128)(2,1)S(1)}, u32[]{:S(2)}, u32[]{:S(2)}) %all-to-all-start) | async-done | bytes 2359328 | tf_op jit(solution)/shard_map/all_to_all | solution.py:188
  72.4 0.9 copy.17
  73.3 0.2 copy.15
  73.5 0.6 gather_fusion
  74.1 0.0 copy-start.1
  74.1 76.9 %shard_map.64 = bf16[384,1536]{1,0:T(8,128)(2,1)S(1)} custom-call(bf16[96,3072]{1,0:T(8,128)(2,1)S(1)} %bitcast.10, bf16[384,1536]{1,0:T(8,128)(2,1)} %q_ref.1), custom_call_target="tpu_custom_call" | custom-call | tf_op jit(solution)/shard_map/pallas_call | solution.py:162
  151.0 0.0 copy-done.1
  151.0 8.8 %add_convert_fusion = bf16[384,3072]{1,0:T(8,128)(2,1)} fusion(bf16[384,3072]{1,0:T(8,128)(2,1)S(1)} %copy-done.1, bf16[384,1536]{1,0:T(8,128)(2,1)S(1)} %shard_map.64, bf16[1536,3072]{1,0:T(8,128)(2,1)} %param.10, pred[384]{0:T(512)(128)(4,1)S(1)} %compare_reduce_fusion), kind=kOutput, calls=%fused_computation.1 | convolution fusion | flops 3630956544 | bytes 15335808 | tf_op jit(solution)/shard_map/dot_general | solution.py:193
  (2 shorter events, 0.0 us)
Async XLA Ops:
  5.6 7.5 %copy-start = (s32[12]{0:T(128)S(1)}, s32[12]{0:T(128)}, u32[]{:S(2)}) copy-start(s32[12]{0:T(128)} %param.11) | copy-start | bytes 148
  5.6 66.9 %all-to-all-start = ((bf16[3,128,3072]{2,0,1:T(4,128)(2,1)}), bf16[3,128,3072]{2,0,1:T(4,128)(2,1)S(1)}, u32[]{:S(2)}, u32[]{:S(2)}) async-start(bf16[3,128,3072]{2,0,1:T(4,128)(2,1)} %copy.13), calls=%async_computation | async-start | bytes 6291456 | tf_op jit(solution)/shard_map/all_to_all | solution.py:188
  74.1 76.9 %copy-start.1 = (bf16[384,3072]{1,0:T(8,128)(2,1)S(1)}, bf16[384,3072]{1,0:T(8,128)(2,1)}, u32[]{:S(2)}) copy-start(bf16[384,3072]{1,0:T(8,128)(2,1)} %param.6) | copy-start | bytes 7077892

commit v3 on v2

v3 whole, which is shorter than its diff:
```python
import functools
import math

import jax
import jax.numpy as jnp
from jax import lax
from jax.experimental import pallas as pl
from jax.experimental.pallas import tpu as pltpu
from jax.sharding import PartitionSpec as P

HEADS = 24
TILE = 128
TILES_DEV = 3
LANES = 128
HALF = 64
ONES = 16
MESH = pl.DeviceIdType.MESH


def ring_device(place, chips, core):
    place = lax.rem(place + chips, chips)
    if chips == 8:
        chip = jnp.where(place < 4, 2 * place, 2 * (7 - place) + 1)
    else:
        chip = place
    return 2 * chip + core


def ring_place(device, chips):
    chip = device // 2
    if chips == 8:
        return jnp.where(lax.rem(chip, 2) == 0, chip // 2, 7 - chip // 2)
    return chip


def attend_kernel(n, tiles_ref, dealt_ref, q_ref, o_ref, got, kv, qs, best, acc, sems):
    deal_send, deal_recv, hop_send, hop_recv, mate_send, mate_recv = sems
    device = lax.axis_index("seq")
    core = lax.rem(device, 2)
    chips = n // 2
    half = chips // 2
    place = ring_place(device, chips)
    sides = (ring_device(place + 1, chips, core), ring_device(place - 1, chips, core))
    mate = device + 1 - 2 * core
    queries, width = q_ref.shape
    pairs = width // LANES
    share_rows = dealt_ref.shape[3]
    rows = kv.shape[1] // chips
    part = rows // 2

    barrier = pltpu.get_barrier_semaphore()
    for away in range(1, n):
        other = lax.rem(device + away, n)
        pl.semaphore_signal(barrier, inc=1, device_id={"seq": other}, device_id_type=MESH)
    pl.semaphore_wait(barrier, n - 1)

    def slot(step):
        return 0 if step == 0 else rows + (step - 1) * 2 * rows

    def region(step, side, chunk):
        base = slot(step) + (rows * side if 0 < step < half else 0)
        return kv.at[core, pl.ds(base + chunk * part, part)]

    def remote(src, dst, send, recv, target):
        copy = pltpu.make_async_remote_copy(
            src_ref=src, dst_ref=dst, send_sem=send, recv_sem=recv,
            device_id={"seq": target}, device_id_type=MESH)
        copy.start()
        return copy

    def hop(step, side, chunk):
        return remote(region(step - 1, side, chunk), region(step, side, chunk), hop_send.at[side, step, chunk],
                      hop_recv.at[side, step, chunk], sides[side])

    def share(step, side, chunk):
        block = region(step, side, chunk)
        return remote(block, block, mate_send.at[side, step, chunk], mate_recv.at[side, step, chunk], mate)

    def compute(start, length, first, low_pair, high_pair):
        def one_pair(h, carry):
            columns = pl.ds(pl.multiple_of(h * LANES, LANES), LANES)
            keys = kv[0, start:start + length, columns]
            values = jnp.transpose(kv[1, start:start + length, columns])
            ones = jnp.ones((ONES, length), jnp.bfloat16)
            both = jnp.dot(keys, qs[h], preferred_element_type=jnp.float32)
            for odd in range(2):
                mine = values[odd * HALF:(odd + 1) * HALF]
                value_one = jnp.concatenate([mine, ones], axis=0)
                scores = both[:, odd * queries:(odd + 1) * queries]
                top = jnp.max(scores, axis=0, keepdims=True)
                if first:
                    weights = jnp.exp(scores - top)
                    acc[h, odd] = jnp.dot(value_one, weights.astype(jnp.bfloat16), preferred_element_type=jnp.float32)
                    best[h, odd] = top
                else:
                    old = best[h, odd]
                    new = jnp.maximum(old, top)
                    weights = jnp.exp(scores - new)
                    more = jnp.dot(value_one, weights.astype(jnp.bfloat16), preferred_element_type=jnp.float32)
                    acc[h, odd] = acc[h, odd] * jnp.exp(old - new) + more
                    best[h, odd] = new
            return carry

        lax.fori_loop(low_pair, high_pair, one_pair, 0, unroll=2)

    def landing(source):
        return got.at[pl.ds(TILES_DEV * source, TILES_DEV)]

    sent = []
    for away in range(n - 1, 0, -1):
        other = lax.rem(device + away, n)
        sent.append(remote(dealt_ref.at[lax.rem(other, 2), other // 2], landing(device), deal_send.at[away],
                           deal_recv.at[away], other))
    local = pltpu.make_async_copy(dealt_ref.at[core, device // 2], landing(device), deal_send.at[0])
    local.start()

    scale = 1.0 / math.sqrt(width // HEADS)

    def split_pair(h, carry):
        columns = pl.ds(pl.multiple_of(h * LANES, LANES), LANES)
        both = jnp.transpose(q_ref[:, columns].astype(jnp.float32) * scale)
        low = lax.broadcasted_iota(jnp.int32, (LANES, 1), 0) < HALF
        qs[h, :, :queries] = jnp.where(low, both, 0.0).astype(jnp.bfloat16)
        qs[h, :, queries:] = jnp.where(low, 0.0, both).astype(jnp.bfloat16)
        return carry

    lax.fori_loop(0, pairs, split_pair, 0)

    local.wait()
    for copy in sent:
        copy.wait_recv()
    for index in range(tiles_ref.shape[0]):
        kv[core, index * share_rows:(index + 1) * share_rows] = got[tiles_ref[index]]

    hops = [[hop(1, side, chunk) for side in range(2)] for chunk in range(2)]
    mates = [share(0, 0, chunk) for chunk in range(2)]
    sent += hops[0] + hops[1] + mates
    for step in range(1, half + 1):
        new_hops, new_mates = [[], []], []
        for chunk in range(2):
            for copy in hops[chunk]:
                copy.wait_recv()
            if step < half - 1:
                new_hops[chunk] = [hop(step + 1, side, chunk) for side in range(2)]
            elif step == half - 1:
                new_hops[chunk] = [hop(half, chunk, chunk)]
            shared = [share(step, side, chunk) for side in range(2 if step < half else 1)]
            sent += new_hops[chunk] + shared
            new_mates += shared
            if chunk == 0:
                for copy in mates:
                    copy.wait_recv()
            compute(slot(step - 1), slot(step) - slot(step - 1), step == 1, chunk * (pairs // 2), (chunk + 1) * (pairs // 2))
        hops, mates = new_hops, new_mates
    for copy in mates:
        copy.wait_recv()
    compute(slot(half), rows, False, 0, pairs)

    def finish(h, carry):
        columns = pl.ds(pl.multiple_of(h * LANES, LANES), LANES)
        done = [acc[h, odd, :HALF] / acc[h, odd, HALF:HALF + 1] for odd in range(2)]
        o_ref[:, columns] = jnp.transpose(jnp.concatenate(done, axis=0)).astype(jnp.bfloat16)
        return carry

    lax.fori_loop(0, pairs, finish, 0)
    for copy in sent:
        copy.wait_send()


def attend(dealt, queries, tiles, n):
    rows, width = queries.shape
    pairs = width // LANES
    half = n // 4
    vmem = pl.BlockSpec(memory_space=pltpu.VMEM)
    share_rows = dealt.shape[3]
    hop_sems = pltpu.SemaphoreType.DMA((2, half + 1, 2))
    return pl.pallas_call(
        functools.partial(attend_kernel, n),
        out_shape=jax.ShapeDtypeStruct((rows, width), jnp.bfloat16),
        in_specs=[pl.BlockSpec(memory_space=pltpu.SMEM), pl.BlockSpec(memory_space=pl.ANY), vmem],
        out_specs=vmem,
        scratch_shapes=[
            pltpu.VMEM((n * TILES_DEV, share_rows, width), jnp.bfloat16),
            pltpu.VMEM((2, tiles.shape[0] * TILE, width), jnp.bfloat16),
            pltpu.VMEM((pairs, LANES, 2 * rows), jnp.bfloat16),
            pltpu.VMEM((pairs, 2, 1, rows), jnp.float32),
            pltpu.VMEM((pairs, 2, HALF + ONES, rows), jnp.float32),
            [pltpu.SemaphoreType.DMA((n,)), pltpu.SemaphoreType.DMA((n,)), hop_sems, hop_sems, hop_sems, hop_sems],
        ],
        compiler_params=pltpu.CompilerParams(
            collective_id=0, has_side_effects=True, vmem_limit_bytes=52 * 1024 * 1024
        ),
    )(tiles, dealt, queries)


def body(hidden, query_rows, key_rows, value_rows, out_weight, masked_tiles):
    n = lax.axis_size("seq")
    device = lax.axis_index("seq")
    tokens, width = key_rows.shape

    def by_chip(field):
        return jnp.transpose(field.reshape(TILES_DEV, n // 2, 2 * TILE // n, width), (1, 0, 2, 3))

    dealt = jnp.stack([by_chip(key_rows), by_chip(value_rows)])
    attended = attend(dealt, query_rows, masked_tiles, n)
    here = device * TILES_DEV + jnp.arange(tokens, dtype=jnp.int32) // TILE
    masked = jnp.any(here[:, None] == masked_tiles[None, :], axis=1)
    residual = jnp.dot(attended, out_weight, preferred_element_type=jnp.float32).astype(jnp.bfloat16)
    residual = jnp.where(masked[:, None], residual, jnp.zeros_like(residual))
    painted = hidden.astype(jnp.float32) + residual.astype(jnp.float32)
    return painted.astype(jnp.bfloat16)


def solution(mesh):
    placed = (
        P(("groups", "seq"), None),
        P(("groups", "seq"), None),
        P(("groups", "seq"), None),
        P(("groups", "seq"), None),
        P(),
        P("groups"),
    )
    return jax.shard_map(
        body, mesh=mesh, in_specs=placed, out_specs=P(("groups", "seq"), None), check_vma=False
    )
```

time: 160 us -> 130 us (0.81)
  waiting for transfers between devices: 59.2 us -> 0 us
  Pallas kernels: 76.9 us -> 118 us
  starting transfers between devices: 7.52 us -> 0 us
  local copies, waits for them, and re-layouts: 5.32 us -> 1.79 us
    all_to_all x1 -> x0, waiting for transfers between devices: 59.2 us -> none  [body(): got = lax.all_to_all(both, 'seq', split_axis=1, concat_axis=0, tiled=True)]
    pallas_call x1, Pallas kernels: 76.9 us -> 118 us  [attend(): pl.pallas_call(functools.partial(attend_kernel, n), out_shape=jax.ShapeDt...]
    all_to_all x1 -> x0, starting transfers between devices: 7.52 us -> none  [body(): got = lax.all_to_all(both, 'seq', split_axis=1, concat_axis=0, tiled=True)]
    reshape x1 -> x0, local copies, waits for them, and re-layouts: 3.68 us -> none  [body(): jnp.concatenate([key_rows, value_rows], axis=1)]
    concatenate x1 -> x0, other arithmetic: 1.87 us -> none  [body(): jnp.concatenate([key_rows, value_rows], axis=1)]
    another operation x0 -> x1, local copies, waits for them, and re-layouts: none -> 1.78 us  [body(): dealt = jnp.stack([by_chip(key_rows), by_chip(value_rows)])]
    another operation x0 -> x1, other arithmetic: none -> 1.61 us  [body(): dealt = jnp.stack([by_chip(key_rows), by_chip(value_rows)])]
  transfers between devices with their start and end apart: 1 -> 0, of which waited for: 1 -> 0; matrix products, arithmetic and copies ran while one was open for 0% -> 0% of each run, Pallas kernels for 0% -> 0%
where the time goes in v3:
time: 130 us
  Pallas kernels  118 us (91%)
  matrix products  8.84 us (7%)
  local copies, waits for them, and re-layouts  1.79 us (1%)
  other arithmetic  1.71 us (1%)
    pallas_call x1, Pallas kernels, attend(): pl.pallas_call(functools.partial(attend_kernel, n), out_shape=jax.ShapeDt...  118 us
    dot_general x1, matrix products, body(): jnp.dot(attended, out_weight, preferred_element_type=jnp.float32)  8.84 us

profile of v3, /device:TPU:0, one launch (start us, length us, event | category | flops | bytes accessed | tf_op | source)
XLA Modules:
  0.0 130.0 jit_solution(3828555563130727768)
XLA Ops:
  0.0 1.8 %copy_bitcast_fusion = (bf16[1,8,3,16,1536]{4,3,2,1,0:T(8,128)(2,1)S(1)}, bf16[1,8,3,16,1536]{4,3,2,1,0:T(8,128)(2,1)S(1)}) fusion(bf16[3,8,16,1536]{3,2,1,0:T(8,128)(2,1)} %bitcast.12, bf16[3,8,16,1536]{3,2,1,0:T(8,128)(2,1)} %bitcast.13), kind=kLoop, calls=%fused_computation.4 | loop fusion | bytes 4718592 | tf_op jit(solution)/shard_map/stack | solution.py:204
  1.8 0.0 copy-start
  1.8 1.6 %pad_maximum_fusion.dealt_ref = bf16[2,8,3,16,1536]{4,3,2,1,0:T(8,128)(2,1)} fusion(bf16[1,8,3,16,1536]{4,3,2,1,0:T(8,128)(2,1)S(1)} %get-tuple-element.5, bf16[1,8,3,16,1536]{4,3,2,1,0:T(8,128)(2,1)S(1)} %get-tuple-element.6), kind=kLoop, calls=%fused_computation.3 | loop fusion | flops 1179648 | bytes 4718592 | tf_op jit(solution)/shard_map/stack | solution.py:204
  3.4 0.0 copy-done
  3.4 0.0 copy-start.1
  3.4 117.6 %shard_map.64 = bf16[384,1536]{1,0:T(8,128)(2,1)S(1)} custom-call(s32[12]{0:T(128)S(1)} %copy-done, bf16[2,8,3,16,1536]{4,3,2,1,0:T(8,128)(2,1)} %pad_maximum_fusion.dealt_ref, bf16[384,1536]{1,0:T(8,128)(2,1)} %q_ref.1), custom_call_target="tpu_custom_call" | custom-call | tf_op jit(solution)/shard_map/pallas_call | solution.py:177
  121.0 0.1 compare_reduce_fusion
  121.1 0.0 copy-done.1
  121.1 8.8 %add_convert_fusion = bf16[384,3072]{1,0:T(8,128)(2,1)} fusion(bf16[384,3072]{1,0:T(8,128)(2,1)S(1)} %copy-done.1, bf16[384,1536]{1,0:T(8,128)(2,1)S(1)} %shard_map.64, bf16[1536,3072]{1,0:T(8,128)(2,1)} %param.10, pred[384]{0:T(512)(128)(4,1)S(1)} %compare_reduce_fusion), kind=kOutput, calls=%fused_computation | convolution fusion | flops 3630956544 | bytes 15335808 | tf_op jit(solution)/shard_map/dot_general | solution.py:208
  (1 shorter events, 0.0 us)
Async XLA Ops:
  1.8 1.6 %copy-start = (s32[12]{0:T(128)S(1)}, s32[12]{0:T(128)}, u32[]{:S(2)}) copy-start(s32[12]{0:T(128)} %tiles_ref.1) | copy-start | bytes 148
  3.4 117.7 %copy-start.1 = (bf16[384,3072]{1,0:T(8,128)(2,1)S(1)}, bf16[384,3072]{1,0:T(8,128)(2,1)}, u32[]{:S(2)}) copy-start(bf16[384,3072]{1,0:T(8,128)(2,1)} %param.6) | copy-start | bytes 7077892

commit v4 on v3

--- a/solution.py
+++ b/solution.py
@@ -57,9 +57,12 @@
     def slot(step):
         return 0 if step == 0 else rows + (step - 1) * 2 * rows
 
-    def region(step, side, chunk):
+    columns_of = [pl.ds(chunk * (width // 2), width // 2) for chunk in range(2)]
+
+    def region(step, side, chunk, last=False):
         base = slot(step) + (rows * side if 0 < step < half else 0)
-        return kv.at[core, pl.ds(base + chunk * part, part)]
+        start, size = (side * part, part) if last else (0, rows)
+        return kv.at[core, pl.ds(base + start, size), columns_of[chunk]]
 
     def remote(src, dst, send, recv, target):
         copy = pltpu.make_async_remote_copy(
@@ -69,7 +72,8 @@
         return copy
 
     def hop(step, side, chunk):
-        return remote(region(step - 1, side, chunk), region(step, side, chunk), hop_send.at[side, step, chunk],
+        last = step == half
+        return remote(region(step - 1, side, chunk, last), region(step, side, chunk, last), hop_send.at[side, step, chunk],
                       hop_recv.at[side, step, chunk], sides[side])
 
     def share(step, side, chunk):
@@ -103,16 +107,20 @@
 
         lax.fori_loop(low_pair, high_pair, one_pair, 0, unroll=2)
 
-    def landing(source):
-        return got.at[pl.ds(TILES_DEV * source, TILES_DEV)]
-
-    sent = []
-    for away in range(n - 1, 0, -1):
-        other = lax.rem(device + away, n)
-        sent.append(remote(dealt_ref.at[lax.rem(other, 2), other // 2], landing(device), deal_send.at[away],
-                           deal_recv.at[away], other))
-    local = pltpu.make_async_copy(dealt_ref.at[core, device // 2], landing(device), deal_send.at[0])
-    local.start()
+    def landing(source, chunk):
+        return got[chunk].at[pl.ds(TILES_DEV * source, TILES_DEV)]
+
+    dealt, local = [[], []], []
+    for chunk in range(2):
+        for away in range(n - 1, 0, -1):
+            other = lax.rem(device + away, n)
+            source = dealt_ref.at[lax.rem(other, 2), other // 2, :, :, columns_of[chunk]]
+            dealt[chunk].append(remote(source, landing(device, chunk), deal_send.at[chunk, away],
+                                       deal_recv.at[chunk, away], other))
+        source = dealt_ref.at[core, device // 2, :, :, columns_of[chunk]]
+        local.append(pltpu.make_async_copy(source, landing(device, chunk), deal_send.at[chunk, 0]))
+        local[chunk].start()
+    sent = dealt[0] + dealt[1]
 
     scale = 1.0 / math.sqrt(width // HEADS)
 
@@ -126,35 +134,34 @@
 
     lax.fori_loop(0, pairs, split_pair, 0)
 
-    local.wait()
-    for copy in sent:
-        copy.wait_recv()
-    for index in range(tiles_ref.shape[0]):
-        kv[core, index * share_rows:(index + 1) * share_rows] = got[tiles_ref[index]]
-
-    hops = [[hop(1, side, chunk) for side in range(2)] for chunk in range(2)]
-    mates = [share(0, 0, chunk) for chunk in range(2)]
-    sent += hops[0] + hops[1] + mates
-    for step in range(1, half + 1):
-        new_hops, new_mates = [[], []], []
+    hops, mates = [[], []], [[], []]
+    skew = 2
+    for time in range(half + 2 + skew):
         for chunk in range(2):
+            step = time - skew * chunk
+            if step < 0 or step > half + 1:
+                continue
+            if step == 0:
+                local[chunk].wait()
+                for copy in dealt[chunk]:
+                    copy.wait_recv()
+                for index in range(tiles_ref.shape[0]):
+                    picked = got[chunk][tiles_ref[index]]
+                    kv[core, index * share_rows:(index + 1) * share_rows, columns_of[chunk]] = picked
+                hops[chunk] = [hop(1, side, chunk) for side in range(2)]
+                mates[chunk] = [share(0, 0, chunk)]
+                sent += hops[chunk] + mates[chunk]
+                continue
             for copy in hops[chunk]:
                 copy.wait_recv()
-            if step < half - 1:
-                new_hops[chunk] = [hop(step + 1, side, chunk) for side in range(2)]
-            elif step == half - 1:
-                new_hops[chunk] = [hop(half, chunk, chunk)]
-            shared = [share(step, side, chunk) for side in range(2 if step < half else 1)]
-            sent += new_hops[chunk] + shared
-            new_mates += shared
-            if chunk == 0:
-                for copy in mates:
-                    copy.wait_recv()
-            compute(slot(step - 1), slot(step) - slot(step - 1), step == 1, chunk * (pairs // 2), (chunk + 1) * (pairs // 2))
-        hops, mates = new_hops, new_mates
-    for copy in mates:
-        copy.wait_recv()
-    compute(slot(half), rows, False, 0, pairs)
+            hops[chunk] = [hop(step + 1, side, chunk) for side in range(2)] if step < half else []
+            shared = [share(step, side, chunk) for side in range(2 if step < half else 1)] if step <= half else []
+            sent += hops[chunk] + shared
+            for copy in mates[chunk]:
+                copy.wait_recv()
+            mates[chunk] = shared
+            length = 2 * rows if 0 < step - 1 < half else rows
+            compute(slot(step - 1), length, step == 1, chunk * (pairs // 2), (chunk + 1) * (pairs // 2))
 
     def finish(h, carry):
         columns = pl.ds(pl.multiple_of(h * LANES, LANES), LANES)
@@ -180,12 +187,12 @@
         in_specs=[pl.BlockSpec(memory_space=pltpu.SMEM), pl.BlockSpec(memory_space=pl.ANY), vmem],
         out_specs=vmem,
         scratch_shapes=[
-            pltpu.VMEM((n * TILES_DEV, share_rows, width), jnp.bfloat16),
+            [pltpu.VMEM((n * TILES_DEV, share_rows, width // 2), jnp.bfloat16)] * 2,
             pltpu.VMEM((2, tiles.shape[0] * TILE, width), jnp.bfloat16),
             pltpu.VMEM((pairs, LANES, 2 * rows), jnp.bfloat16),
             pltpu.VMEM((pairs, 2, 1, rows), jnp.float32),
             pltpu.VMEM((pairs, 2, HALF + ONES, rows), jnp.float32),
-            [pltpu.SemaphoreType.DMA((n,)), pltpu.SemaphoreType.DMA((n,)), hop_sems, hop_sems, hop_sems, hop_sems],
+            [pltpu.SemaphoreType.DMA((2, n)), pltpu.SemaphoreType.DMA((2, n)), hop_sems, hop_sems, hop_sems, hop_sems],
         ],
         compiler_params=pltpu.CompilerParams(
             collective_id=0, has_side_effects=True, vmem_limit_bytes=52 * 1024 * 1024

time: 130 us -> 129 us (level)
  no operation moved by 1% of the time
where the time goes in v4:
time: 129 us
  Pallas kernels  117 us (91%)
  matrix products  8.84 us (7%)
  local copies, waits for them, and re-layouts  1.79 us (1%)
  other arithmetic  1.71 us (1%)
    pallas_call x1, Pallas kernels, attend(): pl.pallas_call(functools.partial(attend_kernel, n), out_shape=jax.ShapeDt...  117 us
    dot_general x1, matrix products, body(): jnp.dot(attended, out_weight, preferred_element_type=jnp.float32)  8.84 us

profile of v4, /device:TPU:0, one launch (start us, length us, event | category | flops | bytes accessed | tf_op | source)
XLA Modules:
  0.0 129.0 jit_solution(6579906284712111784)
XLA Ops:
  0.0 1.8 %copy_bitcast_fusion = (bf16[1,8,3,16,1536]{4,3,2,1,0:T(8,128)(2,1)S(1)}, bf16[1,8,3,16,1536]{4,3,2,1,0:T(8,128)(2,1)S(1)}) fusion(bf16[3,8,16,1536]{3,2,1,0:T(8,128)(2,1)} %bitcast.12, bf16[3,8,16,1536]{3,2,1,0:T(8,128)(2,1)} %bitcast.13), kind=kLoop, calls=%fused_computation.4 | loop fusion | bytes 4718592 | tf_op jit(solution)/shard_map/stack | solution.py:211
  1.8 0.0 copy-start
  1.8 1.6 %pad_maximum_fusion.dealt_ref = bf16[2,8,3,16,1536]{4,3,2,1,0:T(8,128)(2,1)} fusion(bf16[1,8,3,16,1536]{4,3,2,1,0:T(8,128)(2,1)S(1)} %get-tuple-element.5, bf16[1,8,3,16,1536]{4,3,2,1,0:T(8,128)(2,1)S(1)} %get-tuple-element.6), kind=kLoop, calls=%fused_computation.3 | loop fusion | flops 1179648 | bytes 4718592 | tf_op jit(solution)/shard_map/stack | solution.py:211
  3.4 0.0 copy-done
  3.4 0.0 copy-start.1
  3.4 116.7 %shard_map.64 = bf16[384,1536]{1,0:T(8,128)(2,1)S(1)} custom-call(s32[12]{0:T(128)S(1)} %copy-done, bf16[2,8,3,16,1536]{4,3,2,1,0:T(8,128)(2,1)} %pad_maximum_fusion.dealt_ref, bf16[384,1536]{1,0:T(8,128)(2,1)} %q_ref.1), custom_call_target="tpu_custom_call" | custom-call | tf_op jit(solution)/shard_map/pallas_call | solution.py:184
  120.1 0.1 compare_reduce_fusion
  120.2 0.0 copy-done.1
  120.2 8.8 %add_convert_fusion = bf16[384,3072]{1,0:T(8,128)(2,1)} fusion(bf16[384,3072]{1,0:T(8,128)(2,1)S(1)} %copy-done.1, bf16[384,1536]{1,0:T(8,128)(2,1)S(1)} %shard_map.64, bf16[1536,3072]{1,0:T(8,128)(2,1)} %param.10, pred[384]{0:T(512)(128)(4,1)S(1)} %compare_reduce_fusion), kind=kOutput, calls=%fused_computation | convolution fusion | flops 3630956544 | bytes 15335808 | tf_op jit(solution)/shard_map/dot_general | solution.py:215
  (1 shorter events, 0.0 us)
Async XLA Ops:
  1.8 1.6 %copy-start = (s32[12]{0:T(128)S(1)}, s32[12]{0:T(128)}, u32[]{:S(2)}) copy-start(s32[12]{0:T(128)} %tiles_ref.1) | copy-start | bytes 148
  3.4 116.8 %copy-start.1 = (bf16[384,3072]{1,0:T(8,128)(2,1)S(1)}, bf16[384,3072]{1,0:T(8,128)(2,1)}, u32[]{:S(2)}) copy-start(bf16[384,3072]{1,0:T(8,128)(2,1)} %param.6) | copy-start | bytes 7077892

commit v5 on v4

--- a/solution.py
+++ b/solution.py
@@ -33,7 +33,7 @@
     return chip
 
 
-def attend_kernel(n, tiles_ref, dealt_ref, q_ref, o_ref, got, kv, qs, best, acc, sems):
+def attend_kernel(n, tiles_ref, keys_ref, values_ref, q_ref, o_ref, got, kv, qs, best, acc, sems):
     deal_send, deal_recv, hop_send, hop_recv, mate_send, mate_recv = sems
     device = lax.axis_index("seq")
     core = lax.rem(device, 2)
@@ -44,7 +44,7 @@
     mate = device + 1 - 2 * core
     queries, width = q_ref.shape
     pairs = width // LANES
-    share_rows = dealt_ref.shape[3]
+    share_rows = keys_ref.shape[2]
     rows = kv.shape[1] // chips
     part = rows // 2
 
@@ -110,17 +110,43 @@
     def landing(source, chunk):
         return got[chunk].at[pl.ds(TILES_DEV * source, TILES_DEV)]
 
-    dealt, local = [[], []], []
-    for chunk in range(2):
-        for away in range(n - 1, 0, -1):
-            other = lax.rem(device + away, n)
-            source = dealt_ref.at[lax.rem(other, 2), other // 2, :, :, columns_of[chunk]]
-            dealt[chunk].append(remote(source, landing(device, chunk), deal_send.at[chunk, away],
-                                       deal_recv.at[chunk, away], other))
-        source = dealt_ref.at[core, device // 2, :, :, columns_of[chunk]]
-        local.append(pltpu.make_async_copy(source, landing(device, chunk), deal_send.at[chunk, 0]))
-        local[chunk].start()
-    sent = dealt[0] + dealt[1]
+    chip = device // 2
+    fields = (keys_ref, values_ref)
+    sent, arrivals, local = [], [[], []], []
+
+    def to_mate(chunk, kept):
+        source = fields[1 - kept].at[:, chip, :, columns_of[chunk]]
+        return pltpu.make_async_remote_copy(
+            src_ref=source, dst_ref=landing(device, chunk), send_sem=deal_send.at[chunk, 1],
+            recv_sem=deal_recv.at[chunk, 1], device_id={"seq": mate}, device_id_type=MESH)
+
+    def to_self(chunk, kept):
+        source = fields[kept].at[:, chip, :, columns_of[chunk]]
+        return pltpu.make_async_copy(source, landing(device, chunk), deal_send.at[chunk, 0])
+
+    def deal(chunk):
+        for away in range(chips - 1, 0, -1):
+            other = lax.rem(chip + away, chips)
+            for wanted in range(2):
+                source = fields[wanted].at[:, other, :, columns_of[chunk]]
+                send = deal_send.at[chunk, 2 * away + wanted]
+                sent.append(remote(source, landing(device, chunk), send, deal_recv.at[chunk, 2 * away + core],
+                                   2 * other + wanted))
+                arrivals[chunk].append(pltpu.make_async_remote_copy(
+                    src_ref=source, dst_ref=landing(device, chunk), send_sem=send,
+                    recv_sem=deal_recv.at[chunk, 2 * away + wanted],
+                    device_id={"seq": 2 * other + wanted}, device_id_type=MESH))
+        for kept in range(2):
+            @pl.when(core == kept)
+            def _():
+                to_mate(chunk, kept).start()
+                to_self(chunk, kept).start()
+        arrivals[chunk].append(to_mate(chunk, 0))
+        sent.append(arrivals[chunk][-1])
+        local.append(to_self(chunk, 0))
+
+    deal(0)
+    deal(1)
 
     scale = 1.0 / math.sqrt(width // HEADS)
 
@@ -143,7 +169,7 @@
                 continue
             if step == 0:
                 local[chunk].wait()
-                for copy in dealt[chunk]:
+                for copy in arrivals[chunk]:
                     copy.wait_recv()
                 for index in range(tiles_ref.shape[0]):
                     picked = got[chunk][tiles_ref[index]]
@@ -174,17 +200,17 @@
         copy.wait_send()
 
 
-def attend(dealt, queries, tiles, n):
+def attend(keys, values, queries, tiles, n):
     rows, width = queries.shape
     pairs = width // LANES
     half = n // 4
     vmem = pl.BlockSpec(memory_space=pltpu.VMEM)
-    share_rows = dealt.shape[3]
+    share_rows = keys.shape[2]
     hop_sems = pltpu.SemaphoreType.DMA((2, half + 1, 2))
     return pl.pallas_call(
         functools.partial(attend_kernel, n),
         out_shape=jax.ShapeDtypeStruct((rows, width), jnp.bfloat16),
-        in_specs=[pl.BlockSpec(memory_space=pltpu.SMEM), pl.BlockSpec(memory_space=pl.ANY), vmem],
+        in_specs=[pl.BlockSpec(memory_space=pltpu.SMEM), pl.BlockSpec(memory_space=pl.ANY), pl.BlockSpec(memory_space=pl.ANY), vmem],
         out_specs=vmem,
         scratch_shapes=[
             [pltpu.VMEM((n * TILES_DEV, share_rows, width // 2), jnp.bfloat16)] * 2,
@@ -197,7 +223,7 @@
         compiler_params=pltpu.CompilerParams(
             collective_id=0, has_side_effects=True, vmem_limit_bytes=52 * 1024 * 1024
         ),
-    )(tiles, dealt, queries)
+    )(tiles, keys, values, queries)
 
 
 def body(hidden, query_rows, key_rows, value_rows, out_weight, masked_tiles):
@@ -206,10 +232,9 @@
     tokens, width = key_rows.shape
 
     def by_chip(field):
-        return jnp.transpose(field.reshape(TILES_DEV, n // 2, 2 * TILE // n, width), (1, 0, 2, 3))
-
-    dealt = jnp.stack([by_chip(key_rows), by_chip(value_rows)])
-    attended = attend(dealt, query_rows, masked_tiles, n)
+        return field.reshape(TILES_DEV, n // 2, 2 * TILE // n, width)
+
+    attended = attend(by_chip(key_rows), by_chip(value_rows), query_rows, masked_tiles, n)
     here = device * TILES_DEV + jnp.arange(tokens, dtype=jnp.int32) // TILE
     masked = jnp.any(here[:, None] == masked_tiles[None, :], axis=1)
     residual = jnp.dot(attended, out_weight, preferred_element_type=jnp.float32).astype(jnp.bfloat16)

time: 129 us -> 128 us (level)
    another operation x1 -> x0, local copies, waits for them, and re-layouts: 1.78 us -> none  [body(): dealt = jnp.stack([by_chip(key_rows), by_chip(value_rows)])]
    another operation x1 -> x0, other arithmetic: 1.61 us -> none  [body(): dealt = jnp.stack([by_chip(key_rows), by_chip(value_rows)])]
where the time goes in v5:
time: 128 us; the launch traced here: 127 us
  Pallas kernels  117 us (91%)
  matrix products  9.29 us (7%)
    pallas_call x1, Pallas kernels, attend(): pl.pallas_call(functools.partial(attend_kernel, n), out_shape=jax.ShapeDt...  117 us
    dot_general x1, matrix products, body(): jnp.dot(attended, out_weight, preferred_element_type=jnp.float32)  9.29 us

profile of v5, /device:TPU:0, one launch (start us, length us, event | category | flops | bytes accessed | tf_op | source)
XLA Modules:
  0.0 127.4 jit_solution(2676767795220216719)
XLA Ops:
  0.0 0.7 compare_reduce_fusion
  0.7 0.0 copy-start
  0.8 0.7 copy-done
  1.4 0.0 copy-start.1
  1.4 116.7 %shard_map.64 = bf16[384,1536]{1,0:T(8,128)(2,1)S(1)} custom-call(s32[12]{0:T(128)S(1)} %copy-done, bf16[3,8,16,1536]{3,2,1,0:T(8,128)(2,1)} %bitcast.4, bf16[3,8,16,1536]{3,2,1,0:T(8,128)(2,1)} %bitcast.5, bf16[384,1536]{1,0:T(8,128)(2,1)} %q_ref.1), custom_call_target="tpu_custom_call" | custom-call | tf_op jit(solution)/shard_map/pallas_call | solution.py:210
  118.1 0.0 copy-done.1
  118.1 9.3 %add_convert_fusion = bf16[384,3072]{1,0:T(8,128)(2,1)} fusion(bf16[384,3072]{1,0:T(8,128)(2,1)S(1)} %copy-done.1, bf16[384,1536]{1,0:T(8,128)(2,1)S(1)} %shard_map.64, bf16[1536,3072]{1,0:T(8,128)(2,1)} %param.10, pred[384]{0:T(512)(128)(4,1)S(1)} %compare_reduce_fusion), kind=kOutput, calls=%fused_computation | convolution fusion | flops 3630956544 | bytes 15335808 | tf_op jit(solution)/shard_map/dot_general | solution.py:240
  (1 shorter events, 0.0 us)
Async XLA Ops:
  0.7 0.7 copy-start
  1.4 116.7 %copy-start.1 = (bf16[384,3072]{1,0:T(8,128)(2,1)S(1)}, bf16[384,3072]{1,0:T(8,128)(2,1)}, u32[]{:S(2)}) copy-start(bf16[384,3072]{1,0:T(8,128)(2,1)} %param.6) | copy-start | bytes 7077892

commit v6 on v5

--- a/solution.py
+++ b/solution.py
@@ -161,7 +161,7 @@
     lax.fori_loop(0, pairs, split_pair, 0)
 
     hops, mates = [[], []], [[], []]
-    skew = 2
+    skew = 1
     for time in range(half + 2 + skew):
         for chunk in range(2):
             step = time - skew * chunk

time: 128 us -> 127 us (level)
  no operation moved by 1% of the time
where the time goes in v6:
time: 127 us
  Pallas kernels  116 us (91%)
  matrix products  9.29 us (7%)
    pallas_call x1, Pallas kernels, attend(): pl.pallas_call(functools.partial(attend_kernel, n), out_shape=jax.ShapeDt...  116 us
    dot_general x1, matrix products, body(): jnp.dot(attended, out_weight, preferred_element_type=jnp.float32)  9.29 us

profile of v6, /device:TPU:0, one launch (start us, length us, event | category | flops | bytes accessed | tf_op | source)
XLA Modules:
  0.0 126.9 jit_solution(14895699625901857525)
XLA Ops:
  0.0 0.7 compare_reduce_fusion
  0.7 0.0 copy-start
  0.8 0.7 copy-done
  1.4 0.0 copy-start.1
  1.4 116.2 %shard_map.64 = bf16[384,1536]{1,0:T(8,128)(2,1)S(1)} custom-call(s32[12]{0:T(128)S(1)} %copy-done, bf16[3,8,16,1536]{3,2,1,0:T(8,128)(2,1)} %bitcast.4, bf16[3,8,16,1536]{3,2,1,0:T(8,128)(2,1)} %bitcast.5, bf16[384,1536]{1,0:T(8,128)(2,1)} %q_ref.1), custom_call_target="tpu_custom_call" | custom-call | tf_op jit(solution)/shard_map/pallas_call | solution.py:210
  117.7 0.0 copy-done.1
  117.7 9.3 %add_convert_fusion = bf16[384,3072]{1,0:T(8,128)(2,1)} fusion(bf16[384,3072]{1,0:T(8,128)(2,1)S(1)} %copy-done.1, bf16[384,1536]{1,0:T(8,128)(2,1)S(1)} %shard_map.64, bf16[1536,3072]{1,0:T(8,128)(2,1)} %param.10, pred[384]{0:T(512)(128)(4,1)S(1)} %compare_reduce_fusion), kind=kOutput, calls=%fused_computation | convolution fusion | flops 3630956544 | bytes 15335808 | tf_op jit(solution)/shard_map/dot_general | solution.py:240
  (1 shorter events, 0.0 us)
Async XLA Ops:
  0.7 0.7 copy-start
  1.4 116.2 %copy-start.1 = (bf16[384,3072]{1,0:T(8,128)(2,1)S(1)}, bf16[384,3072]{1,0:T(8,128)(2,1)}, u32[]{:S(2)}) copy-start(bf16[384,3072]{1,0:T(8,128)(2,1)} %param.6) | copy-start | bytes 7077892
